TPU v7x, 32 devices: a whole 2x2x4 slice. The times are simulated.
32 devices in a mesh: batch: 8 (over z, core), ctx: 4 (over y, x).
Axes of the slice: x: 2, y: 2, z: 4, core: 2. Of those that a mesh axis runs over, the one named last changes fastest.
Arguments:
- tokens: bfloat16 [8, 512, 2048], P('batch', 'ctx'), may hold values from -6 to 6
- out_grad: bfloat16 [8, 512, 2048], P('batch', 'ctx'), may hold values from -6 to 6
- ln1_gain: bfloat16 [2048], P(('batch', 'ctx')), may hold values from 0.5 to 1.5
- ln1_shift: bfloat16 [2048], P(('batch', 'ctx')), may hold values from -3 to 3
- qkv_weight: bfloat16 [2048, 6144], P(('batch', 'ctx')), may hold values from -0.125 to 0.125
- qkv_bias: bfloat16 [6144], P(('batch', 'ctx')), may hold values from -3 to 3
- out_weight: bfloat16 [2048, 2048], P(('batch', 'ctx')), may hold values from -1 to 1
- ln2_gain: bfloat16 [2048], P(('batch', 'ctx')), may hold values from 0.5 to 1.5
- ln2_shift: bfloat16 [2048], P(('batch', 'ctx')), may hold values from -3 to 3
- gate_weight: bfloat16 [2048, 5632], P(('batch', 'ctx')), may hold values from -0.125 to 0.125
- up_weight: bfloat16 [2048, 5632], P(('batch', 'ctx')), may hold values from -0.125 to 0.125
- down_weight: bfloat16 [2048, 5632], P(('batch', 'ctx')), may hold values from -0.078125 to 0.078125
Outputs:
- mixed: bfloat16 [8, 512, 2048], P('batch', 'ctx')
- tokens_grad: float32 [8, 512, 2048], P('batch', 'ctx')
- ln1_gain_grad: float32 [2048], P(('batch', 'ctx'))
- ln1_shift_grad: float32 [2048], P(('batch', 'ctx'))
- qkv_weight_grad: float32 [2048, 6144], P(('batch', 'ctx'))
- qkv_bias_grad: float32 [6144], P(('batch', 'ctx'))
- out_weight_grad: float32 [2048, 2048], P(('batch', 'ctx'))
- ln2_gain_grad: float32 [2048], P(('batch', 'ctx'))
- ln2_shift_grad: float32 [2048], P(('batch', 'ctx'))
- gate_weight_grad: float32 [2048, 5632], P(('batch', 'ctx'))
- up_weight_grad: float32 [2048, 5632], P(('batch', 'ctx'))
- down_weight_grad: float32 [2048, 5632], P(('batch', 'ctx'))
All inputs are finite; a program needn't handle non-finite values.
Results may differ from a plain program's by a relative error of at most 0.03.
Values may be sent and summed in bfloat16 or wider, within the bound.
A program may use at most 576 MiB of HBM per device.

v0:
```python
import functools

import jax
import jax.numpy as jnp
import numpy as np
from jax import lax
from jax.experimental import pallas as pl
from jax.experimental.pallas import tpu as pltpu
from jax.sharding import PartitionSpec as P

D = 2048
FF = 5632
H = 32
HD = 64
ROT = 16


def layer_norm(values, gain, shift):
    centre = jnp.mean(values, axis=-1, keepdims=True)
    centred = values - centre
    spread = jnp.mean(centred * centred, axis=-1, keepdims=True)
    return centred * lax.rsqrt(spread + 1e-05) * gain + shift


def rotary(values, positions):
    half_dims = ROT // 2
    frequency = 10000.0 ** (-jnp.arange(half_dims, dtype=jnp.float32) * 2.0 / ROT)
    angles = positions.astype(jnp.float32)[:, None] * frequency[None, :]
    cosine_term = jnp.cos(angles)[:, None, :]
    sine_term = jnp.sin(angles)[:, None, :]
    first_half = values[..., :half_dims]
    second_half = values[..., half_dims:ROT]
    return jnp.concatenate(
        [
            first_half * cosine_term - second_half * sine_term,
            second_half * cosine_term + first_half * sine_term,
            values[..., ROT:],
        ],
        axis=-1,
    )


def swish_product(gate_value, up_value):
    return gate_value / (1.0 + jnp.exp(-gate_value)) * up_value


def project_back(left, right):
    return lax.dot_general(
        left, right, (((1,), (1,)), ((), ())), preferred_element_type=jnp.float32
    )


def outer_rows(left, right):
    return lax.dot_general(
        left, right, (((0,), (0,)), ((), ())), preferred_element_type=jnp.float32
    )


def local(
    tokens,
    out_grad,
    ln1_gain,
    ln1_shift,
    qkv_weight,
    qkv_bias,
    out_weight,
    ln2_gain,
    ln2_shift,
    gate_weight,
    up_weight,
    down_weight,
):
    local_rows = tokens.shape[1]
    seq_length = local_rows * lax.axis_size("ctx")
    inputs = tokens.reshape(local_rows, D).astype(jnp.float32)
    cotangent = out_grad.reshape(local_rows, D).astype(jnp.float32)
    places = lax.axis_index("ctx") * local_rows + jnp.arange(local_rows, dtype=jnp.int32)
    attn_set = (
        lax.all_gather(qkv_weight, ("batch", "ctx"), axis=0, tiled=True),
        lax.all_gather(out_weight, ("batch", "ctx"), axis=0, tiled=True),
        lax.all_gather(qkv_bias, ("batch", "ctx"), axis=0, tiled=True),
        lax.all_gather(ln1_gain, ("batch", "ctx"), axis=0, tiled=True),
        lax.all_gather(ln1_shift, ("batch", "ctx"), axis=0, tiled=True),
    )
    gain_one = attn_set[3].astype(jnp.float32)
    shift_one = attn_set[4].astype(jnp.float32)
    normed = layer_norm(inputs, gain_one, shift_one)
    normed_low = normed.astype(jnp.bfloat16)
    projected = jnp.dot(normed_low, attn_set[0], preferred_element_type=jnp.float32) + attn_set[
        2
    ].astype(jnp.float32)
    pair_heads = projected[:, : 2 * D].reshape(local_rows, 2 * H, HD)
    turned = rotary(pair_heads, places)
    queries = turned[:, :H].astype(jnp.bfloat16)
    key_rows = turned[:, H:].reshape(local_rows, D).astype(jnp.bfloat16)
    value_rows = projected[:, 2 * D :].astype(jnp.bfloat16)
    start_state = (
        jnp.full((H, local_rows), -1e30, jnp.float32),
        jnp.zeros((H, local_rows), jnp.float32),
        jnp.zeros((H, local_rows, HD), jnp.float32),
    )
    carry = start_state
    key_piece = lax.all_gather(key_rows, "ctx", axis=0, tiled=True)
    value_piece = lax.all_gather(value_rows, "ctx", axis=0, tiled=True)
    piece_rows = key_piece.shape[0]
    block_rows = 512
    block_count = piece_rows // block_rows

    def inner(state, block):
        largest, totals, accum = state
        key_block, value_block, offset = block
        raw_scores = (
            jnp.einsum("qhd,khd->hqk", queries, key_block, preferred_element_type=jnp.float32)
            * 0.125
        )
        key_places = offset + jnp.arange(block_rows, dtype=jnp.int32)
        allowed = (key_places[None, :] <= places[:, None])[None]
        raw_scores = jnp.where(allowed, raw_scores, -1e30)
        new_largest = jnp.maximum(largest, jnp.max(raw_scores, axis=-1))
        weights = jnp.where(allowed, jnp.exp(raw_scores - new_largest[..., None]), 0.0)
        factor = jnp.exp(largest - new_largest)
        totals = totals * factor + jnp.sum(weights, axis=-1)
        accum = accum * factor[..., None] + jnp.einsum(
            "hqk,khd->hqd",
            weights.astype(jnp.bfloat16),
            value_block,
            preferred_element_type=jnp.float32,
        )
        return ((new_largest, totals, accum), None)

    offsets = jnp.arange(block_count, dtype=jnp.int32) * block_rows
    blocks = (
        key_piece.reshape(block_count, block_rows, H, HD),
        value_piece.reshape(block_count, block_rows, H, HD),
        offsets,
    )
    carry, unused = lax.scan(inner, carry, blocks)
    largest, totals, accum = carry
    attended = jnp.transpose(accum / totals[..., None], (1, 0, 2)).reshape(local_rows, D)
    log_total = largest + jnp.log(totals)
    attended_low = attended.astype(jnp.bfloat16)
    middle = inputs + jnp.dot(attended_low, attn_set[1], preferred_element_type=jnp.float32)
    mlp_set = (
        lax.all_gather(gate_weight, ("batch", "ctx"), axis=0, tiled=True),
        lax.all_gather(up_weight, ("batch", "ctx"), axis=0, tiled=True),
        lax.all_gather(down_weight, ("batch", "ctx"), axis=0, tiled=True),
        lax.all_gather(ln2_gain, ("batch", "ctx"), axis=0, tiled=True),
        lax.all_gather(ln2_shift, ("batch", "ctx"), axis=0, tiled=True),
    )
    gain_two = mlp_set[3].astype(jnp.float32)
    shift_two = mlp_set[4].astype(jnp.float32)
    normed_two_low = layer_norm(middle, gain_two, shift_two).astype(jnp.bfloat16)
    gate_value = jnp.dot(normed_two_low, mlp_set[0], preferred_element_type=jnp.float32)
    up_value = jnp.dot(normed_two_low, mlp_set[1], preferred_element_type=jnp.float32)
    hidden_low = swish_product(gate_value, up_value).astype(jnp.bfloat16)
    mixed = (middle + project_back(hidden_low, mlp_set[2])).astype(jnp.bfloat16)
    mlp_back = (
        lax.all_gather(gate_weight, ("batch", "ctx"), axis=0, tiled=True),
        lax.all_gather(up_weight, ("batch", "ctx"), axis=0, tiled=True),
        lax.all_gather(down_weight, ("batch", "ctx"), axis=0, tiled=True),
        lax.all_gather(ln2_gain, ("batch", "ctx"), axis=0, tiled=True),
        lax.all_gather(ln2_shift, ("batch", "ctx"), axis=0, tiled=True),
    )
    attn_back = (
        lax.all_gather(qkv_weight, ("batch", "ctx"), axis=0, tiled=True),
        lax.all_gather(out_weight, ("batch", "ctx"), axis=0, tiled=True),
        lax.all_gather(qkv_bias, ("batch", "ctx"), axis=0, tiled=True),
        lax.all_gather(ln1_gain, ("batch", "ctx"), axis=0, tiled=True),
        lax.all_gather(ln1_shift, ("batch", "ctx"), axis=0, tiled=True),
    )
    branch_two = cotangent.astype(jnp.bfloat16)
    hidden_grad = jnp.dot(branch_two, mlp_back[2], preferred_element_type=jnp.float32)
    unused_value, act_pull = jax.vjp(swish_product, gate_value, up_value)
    gate_grad, up_grad = act_pull(hidden_grad)
    gate_low = gate_grad.astype(jnp.bfloat16)
    up_low = up_grad.astype(jnp.bfloat16)
    normed_two_grad = project_back(gate_low, mlp_back[0]) + project_back(up_low, mlp_back[1])
    unused_two, norm_pull_two = jax.vjp(layer_norm, middle, gain_two, shift_two)
    middle_part, gain_two_grad, shift_two_grad = norm_pull_two(normed_two_grad)
    middle_grad = cotangent + middle_part
    gate_weight_grad, up_weight_grad, down_weight_grad = (
        lax.psum_scatter(
            outer_rows(left, right).astype(jnp.bfloat16), ("batch", "ctx"), scatter_dimension=0, tiled=True
        ).astype(jnp.float32)
        for left, right in ((normed_two_low, gate_low), (normed_two_low, up_low), (branch_two, hidden_low))
    )
    branch_one = middle_grad.astype(jnp.bfloat16)
    out_term = outer_rows(attended_low, branch_one)
    attended_grad = project_back(branch_one, attn_back[1]).astype(jnp.bfloat16)
    grad_heads = attended_grad.reshape(local_rows, H, HD)
    delta = jnp.transpose(
        jnp.sum((attended_grad.astype(jnp.float32) * attended).reshape(local_rows, H, HD), axis=-1)
    )
    key_all, value_all = (
        lax.all_gather(key_rows, "ctx", axis=0, tiled=True),
        lax.all_gather(value_rows, "ctx", axis=0, tiled=True),
    )
    back_rows = 512
    back_count = seq_length // back_rows

    def back_block(query_grad, block):
        key_block, value_block, offset = block
        raw_scores = (
            jnp.einsum("qhd,khd->hqk", queries, key_block, preferred_element_type=jnp.float32)
            * 0.125
        )
        key_places = offset + jnp.arange(back_rows, dtype=jnp.int32)
        allowed = (key_places[None, :] <= places[:, None])[None]
        probs = jnp.where(allowed, jnp.exp(raw_scores - log_total[..., None]), 0.0)
        prob_grad = jnp.einsum(
            "qhd,khd->hqk", grad_heads, value_block, preferred_element_type=jnp.float32
        )
        score_grad = (probs * (prob_grad - delta[..., None])).astype(jnp.bfloat16)
        query_grad = (
            query_grad
            + jnp.einsum("hqk,khd->qhd", score_grad, key_block, preferred_element_type=jnp.float32)
            * 0.125
        )
        key_grad = (
            jnp.einsum("hqk,qhd->khd", score_grad, queries, preferred_element_type=jnp.float32)
            * 0.125
        )
        value_grad = jnp.einsum(
            "hqk,qhd->khd",
            probs.astype(jnp.bfloat16),
            grad_heads,
            preferred_element_type=jnp.float32,
        )
        return (
            query_grad,
            jnp.concatenate(
                [key_grad.reshape(back_rows, D), value_grad.reshape(back_rows, D)], axis=1
            ),
        )

    back_offsets = jnp.arange(back_count, dtype=jnp.int32) * back_rows
    back_blocks = (
        key_all.reshape(back_count, back_rows, H, HD),
        value_all.reshape(back_count, back_rows, H, HD),
        back_offsets,
    )
    query_grad, kv_terms = lax.scan(
        back_block, jnp.zeros((local_rows, H, HD), jnp.float32), back_blocks
    )
    kv_local = lax.psum_scatter(
        kv_terms.reshape(seq_length, 2 * D).astype(jnp.bfloat16),
        "ctx",
        scatter_dimension=0,
        tiled=True,
    ).astype(jnp.float32)

    def turn_heads(heads_in):
        return rotary(heads_in, places)

    unused_three, turn_pull = jax.vjp(turn_heads, pair_heads)
    pair_grad = turn_pull(
        jnp.concatenate([query_grad, kv_local[:, :D].reshape(local_rows, H, HD)], axis=1)
    )[0]
    projected_grad = jnp.concatenate(
        [pair_grad.reshape(local_rows, 2 * D), kv_local[:, D:]], axis=1
    ).astype(jnp.bfloat16)
    qkv_term = outer_rows(normed_low, projected_grad)
    bias_term = jnp.sum(projected_grad.astype(jnp.float32), axis=0)
    normed_grad = project_back(projected_grad, attn_back[0])
    unused_four, norm_pull = jax.vjp(layer_norm, inputs, gain_one, shift_one)
    input_part, gain_one_grad, shift_one_grad = norm_pull(normed_grad)
    tokens_grad = (middle_grad + input_part).reshape(1, local_rows, D)
    summed = (
        lax.psum_scatter(qkv_term, ("batch", "ctx"), scatter_dimension=0, tiled=True),
        lax.psum_scatter(out_term, ("batch", "ctx"), scatter_dimension=0, tiled=True),
        lax.psum_scatter(bias_term, ("batch", "ctx"), scatter_dimension=0, tiled=True),
        lax.psum_scatter(gain_one_grad, ("batch", "ctx"), scatter_dimension=0, tiled=True),
        lax.psum_scatter(shift_one_grad, ("batch", "ctx"), scatter_dimension=0, tiled=True),
        lax.psum_scatter(gain_two_grad, ("batch", "ctx"), scatter_dimension=0, tiled=True),
        lax.psum_scatter(shift_two_grad, ("batch", "ctx"), scatter_dimension=0, tiled=True),
    )
    return (
        mixed.reshape(1, local_rows, D),
        tokens_grad,
        summed[3],
        summed[4],
        summed[0],
        summed[2],
        summed[1],
        summed[5],
        summed[6],
        gate_weight_grad,
        up_weight_grad,
        down_weight_grad,
    )


BF = jnp.bfloat16
F32 = jnp.float32
MESH = pl.DeviceIdType.MESH
ANY = pl.ANY
VM = pltpu.VMEM
REMOTE_SEMS = 240
LOCAL_SEMS = 64


def nt(left, right):
    return lax.dot_general(left, right, (((1,), (1,)), ((), ())), preferred_element_type=F32)


def tn(left, right):
    return lax.dot_general(left, right, (((0,), (0,)), ((), ())), preferred_element_type=F32)


def nn(left, right):
    return jnp.dot(left, right, preferred_element_type=F32)


def norm_stats(values):
    centre = jnp.mean(values, axis=-1, keepdims=True)
    centred = values - centre
    spread = jnp.mean(centred * centred, axis=-1, keepdims=True)
    scale = lax.rsqrt(spread + 1e-05)
    return centred * scale, scale


def norm_back(grad, unit, scale, gain):
    weighted = grad * gain
    lead = jnp.mean(weighted, axis=-1, keepdims=True)
    tilt = jnp.mean(weighted * unit, axis=-1, keepdims=True)
    return scale * (weighted - lead - unit * tilt)


def turn_tables(length):
    half = ROT // 2
    freq = (np.float32(10000.0) ** (-np.arange(half, dtype=np.float32) * np.float32(2.0) / np.float32(ROT))).astype(np.float32)
    angles = np.arange(length, dtype=np.float32)[:, None] * freq[None, :]
    cosine, sine = np.cos(angles), np.sin(angles)
    tables = np.zeros((2, length, 128), np.float32)
    tables[0] = 1.0
    for start in (0, HD):
        tables[0, :, start : start + half] = cosine
        tables[0, :, start + half : start + ROT] = cosine
        tables[1, :, start : start + half] = -sine
        tables[1, :, start + half : start + ROT] = sine
    return tables


def aligned(value, to):
    return value if isinstance(value, int) else pl.multiple_of(value, to)


def feed_columns(width):
    return 2 * width + -(-width // 128) * 128


class Names:
    pass


def layer_kernel(dims, names_in, names_out, names_scratch, *refs):
    R, C, PL, rows, shard, QW, FW, PARTS = dims
    r = Names()
    for name, ref in zip(names_in + names_out + names_scratch, refs):
        setattr(r, name, ref)
    batch = lax.axis_index("batch")
    c = lax.axis_index("ctx")
    z = batch // 2
    core = lax.rem(batch, 2)
    q = core * C + c
    HS = PL // 2 * rows
    TOK = PL * rows
    KB = PL * shard
    STARTS = [sum(PARTS[:p]) for p in range(len(PARTS))]
    WC = [feed_columns(width) for width in PARTS]

    at_plane = [z == at for at in range(R)]
    counter = [0]
    local_count = [0]

    def slots(count):
        first = counter[0]
        counter[0] += count
        return first

    def mate(i):
        other = lax.rem(q + i, PL)
        return (z * 2 + other // C, lax.rem(other, C))

    def row_index(i):
        across, along = lax.rem(lax.rem(c, 2) + lax.rem(i, 2), 2), lax.rem(c // 2 + i // 2, 2)
        return 2 * along + across

    def row_mate(i):
        return (batch, row_index(i))

    sibling = (z * 2 + 1 - core, c)

    def plane_dev(t):
        return (t * 2 + core, c)

    def rcopy(src, dst, send, recv, dev):
        return pltpu.make_async_remote_copy(
            src_ref=src, dst_ref=dst, send_sem=r.ss.at[send], recv_sem=r.rs.at[recv], device_id=dev, device_id_type=MESH
        )

    drains = []

    def lcopy(src, dst):
        copy = pltpu.make_async_copy(src, dst, r.ls.at[local_count[0]])
        local_count[0] += 1
        copy.start()
        return copy

    loads = {name: lcopy(getattr(r, "in_" + name), getattr(r, "v_" + name)) for name in ("tokens", "cot")}

    local_tables = lcopy(r.tables, r.turns)
    barrier = pltpu.get_barrier_semaphore()
    for i in range(1, PL):
        pl.semaphore_signal(barrier, inc=1, device_id=mate(i), device_id_type=MESH)
    for i in range(1, R):
        pl.semaphore_signal(barrier, inc=1, device_id=plane_dev(lax.rem(z + i, R)), device_id_type=MESH)
    pl.semaphore_wait(barrier, PL - 1 + R - 1)

    OFFS = (2, -2, 1, -1)

    class ZGather:
        def __init__(self, whole, height, chunks=1):
            self.whole, self.height, self.chunks = whole, height, chunks
            self.base = [slots(6) for _ in range(chunks)]

        def block(self, s, chunk=None):
            if chunk is None:
                return self.whole.at[pl.ds(aligned(s * self.height, 16), self.height)]
            part = self.height // self.chunks
            return self.whole.at[pl.ds(aligned(s * self.height + chunk * part, 16), part)]

        def guarded(self, ok, make):
            @pl.when(ok)
            def _():
                make().start()

            def drain():
                @pl.when(ok)
                def _():
                    make().wait_send()

            drains.append(drain)

        def start(self, src=None):
            for chunk in range(self.chunks):
                for k, off in enumerate(OFFS):
                    t = z + off
                    ok = (t >= 0) & (t < R)
                    if off == 2:
                        ok = ok & (z == 0)
                    if off == -2:
                        ok = ok & (z == R - 1)

                    def make(chunk=chunk, k=k, t=t):
                        mine = self.block(z, chunk)
                        return rcopy(mine if src is None else src, mine, self.base[chunk] + k, self.base[chunk] + z, plane_dev(t))

                    self.guarded(ok, make)

        def got(self, s, chunk):
            block = self.block(s, chunk)
            rcopy(block, block, self.base[chunk], self.base[chunk] + s, sibling).wait_recv()

        def relay(self, chunk=0):
            for at, blocks, to in ((R - 2, (1, 0), R - 1), (1, (2, 3), 0)):
                for k, s in enumerate(blocks):

                    @pl.when(z == at)
                    def _():
                        self.got(s, chunk)

                    def make(s=s, to=to, k=k):
                        block = self.block(s, chunk)
                        return rcopy(block, block, self.base[chunk] + 4 + k, self.base[chunk] + s, plane_dev(to))

                    self.guarded(z == at, make)

        def wait_block(self, s):
            for chunk in range(self.chunks):
                skip = z == s
                skip = skip | (z == (R - 2 if s < 2 else 1))

                @pl.when(jnp.logical_not(skip))
                def _():
                    self.got(s, chunk)

        def wait(self):
            for s in range(R):
                self.wait_block(s)

    class Spread:
        def __init__(self, stage):
            self.stage, self.base = stage, slots(PL)

        def start(self, target):
            self.target = target
            for i in range(1, PL):
                other = lax.rem(q + i, PL)
                copy = rcopy(self.stage.at[other], target, self.base + i, self.base + i, mate(i))
                copy.start()

        def wait_send(self):
            for i in range(1, PL):
                other = lax.rem(q + i, PL)
                rcopy(self.stage.at[other], self.target, self.base + i, self.base + i, mate(i)).wait_send()

        def wait(self, block):
            for i in range(1, PL):
                rcopy(self.stage.at[0], block(lax.rem(q - i + PL, PL)), self.base + i, self.base + i, mate(i)).wait_recv()

    class Gather:
        def __init__(self, whole):
            self.whole, self.base = whole, slots(2 * C)

        def block(self, s):
            return self.whole.at[pl.ds(aligned(s * rows, 16), rows)]

        def start(self, src):
            self.local = lcopy(src, self.block(q))
            sends = []
            for i in range(1, C):
                sends.append(rcopy(src, self.block(q), self.base + i, self.base + i, row_mate(i)))
            sends.append(rcopy(src, self.block(q), self.base, self.base, sibling))
            for copy in sends:
                copy.start()
            self.sends = sends

        def drain(self):
            for copy in self.sends:
                copy.wait_send()
            for i in range(1, C):
                self.passed(i).wait_send()

        def relay(self):
            for i in range(1, C):
                self.relay_one(i)

        def passed(self, i):
            block = self.block(core * C + row_index(i))
            return rcopy(block, block, self.base + C - 1 + i, self.base + C - 1 + i, sibling)

        def relay_one(self, i):
            block = self.block(core * C + row_index(i))
            rcopy(block, block, self.base, self.base + i, sibling).wait_recv()
            self.passed(i).start()

        def wait_one(self, i):
            block = self.block((1 - core) * C + row_index(i))
            sem = self.base + jnp.where(i == 0, 0, C - 1 + i)
            rcopy(block, block, self.base, sem, sibling).wait_recv()

        def wait(self):
            for i in range(C):
                self.wait_one(i)
            self.local.wait()

        def each(self, use):
            self.local.wait()

            @pl.loop(0, C)
            def _(i):
                @pl.when(i > 0)
                def _():
                    self.relay_one(i)

                use(core * C + row_index(i))
                self.wait_one(i)
                use((1 - core) * C + row_index(i))

    class Reduce:
        def __init__(self, k, before=None):
            self.sibout, self.theirs = getattr(r, f"sibout{k}"), getattr(r, f"theirs{k}")
            self.out, self.got, self.own = getattr(r, f"redout{k}"), getattr(r, f"redin{k}"), getattr(r, f"redown{k}")
            self.base = slots(C + 2)
            self.before = before


        def run(self, pairs, compute, later=False):
            chunk_rows = HS // 2

            def to_sibling(chunk):
                span = pl.ds(chunk * chunk_rows, chunk_rows)
                return rcopy(self.sibout.at[span], self.theirs.at[span], self.base + C + chunk, self.base + C + chunk, sibling)

            def product(target, weights, seq, chunk):
                total = None
                for (x, _), w in zip(pairs, weights):
                    term = compute(x[pl.ds(aligned(seq * HS + chunk * chunk_rows, 16), chunk_rows), :], w)
                    total = term if total is None else total + term
                target[chunk * chunk_rows : (chunk + 1) * chunk_rows, :] = total.astype(BF)

            def pass_on(chunk):
                to_sibling(chunk).wait_recv()
                for blk in range(chunk * C // 2, (chunk + 1) * C // 2):
                    i = lax.rem(blk + c, 2) + 2 * lax.rem(blk // 2 + c // 2, 2)
                    span = pl.ds(blk * rows, rows)
                    total = r.mine[span, :].astype(F32) + self.theirs[span, :].astype(F32)

                    @pl.when(i == 0)
                    def _():
                        self.own[...] = total.astype(self.own.dtype)

                    @pl.when(i != 0)
                    def _():
                        self.out[i - 1] = total.astype(BF)
                        self.to_row(i, blk).start()

            def body(*bufs):
                bufs = list(bufs)
                weights, loads = [], []
                for _, w in pairs:
                    if isinstance(w, tuple):
                        weights.append(bufs.pop(0))
                        loads.append(lcopy(w[0], weights[-1]))
                    else:
                        weights.append(w)
                for load in loads:
                    load.wait()
                if self.before is not None:
                    self.before.drain()
                product(self.sibout, weights, 1 - core, 0)
                to_sibling(0).start()
                product(r.mine, weights, core, 0)
                product(self.sibout, weights, 1 - core, 1)
                to_sibling(1).start()
                if not later:
                    pass_on(0)
                product(r.mine, weights, core, 1)
                if not later:
                    pass_on(1)

            pl.run_scoped(body, *[VM(w[0].shape, BF) for _, w in pairs if isinstance(w, tuple)])
            self.drain = lambda: self.drain_all(to_sibling)
            self.pass_on = lambda: (pass_on(0), pass_on(1))

        def to_row(self, i, blk):
            return rcopy(self.out.at[i - 1], self.got.at[i - 1], self.base + i, self.base + i, (batch, blk))

        def drain_all(self, to_sibling):
            to_sibling(0).wait_send()
            to_sibling(1).wait_send()
            for i in range(1, C):
                self.to_row(i, row_index(i)).wait_send()

        def finish(self):
            for i in range(1, C):
                rcopy(self.out.at[i - 1], self.got.at[i - 1], self.base + i, self.base + i, row_mate(i)).wait_recv()
            total = self.own[...].astype(F32)
            for i in range(1, C):
                total = total + self.got[i - 1].astype(F32)
            return total

    ORDER = ((3, 2, 1, 0), (0, 3, 2, 1), (3, 0, 1, 2), (0, 1, 2, 3))

    class ZReduce:
        def __init__(self, grads, got, extra, merged, height):
            self.grads, self.got, self.extra, self.merged, self.height = grads, got, extra, merged, height
            self.base = slots(12)

        def block(self, t):
            return self.grads.at[pl.ds(aligned(t * self.height, 16), self.height)]

        def guarded(self, ok, make):
            @pl.when(ok)
            def _():
                make().start()

            def drain():
                @pl.when(ok)
                def _():
                    make().wait_send()

            drains.append(drain)

        def send(self, at, owner):
            b = self.base
            via = {0: 1, R - 1: R - 2}.get(at)
            if owner == at or (via is None and abs(owner - at) == 2) or (via is None and owner == R - 1 - at):
                return
            if via is None:
                slot = 1 if owner < at else 0
                make = lambda: rcopy(self.block(owner), self.got.at[slot], b + 3, b + slot, plane_dev(owner))
            elif owner == via:
                slot = 0 if at == 0 else 1
                make = lambda: rcopy(self.block(owner), self.got.at[slot], b + 2, b + slot, plane_dev(via))
            else:
                k = 0 if owner == R - 1 - at else 1
                make = lambda: rcopy(self.block(owner), self.extra.at[k], b + k, b + 2 + k, plane_dev(via))
            self.guarded(at_plane[at], make)

        def start(self):
            for step in range(R):
                self.start_step(step)

        def start_step(self, step):
            for at in range(R):
                self.send(at, ORDER[at][step])

        def merge(self, steps=(0, 1)):
            b = self.base
            for k in steps:
                for at, to, slots_at in ((1, (3, 2), (1, 0)), (2, (0, 1), (0, 1))):
                    owner = to[k]

                    @pl.when(z == at)
                    def _():
                        def body(own, other, sem):
                            first = pltpu.make_async_copy(self.block(owner), own, sem.at[0])
                            first.start()
                            rcopy(self.extra.at[k], self.extra.at[k], b, b + 2 + k, sibling).wait_recv()
                            second = pltpu.make_async_copy(self.extra.at[k], other, sem.at[1])
                            second.start()
                            first.wait()
                            second.wait()
                            own[...] = (own[...].astype(F32) + other[...].astype(F32)).astype(BF)
                            pltpu.sync_copy(own, self.merged.at[k])

                        shape = (self.height, self.grads.shape[1])
                        pl.run_scoped(body, VM(shape, BF), VM(shape, BF), pltpu.SemaphoreType.DMA((2,)))

                    self.guarded(
                        z == at,
                        lambda k=k, owner=owner, slot=slots_at[k]: rcopy(
                            self.merged.at[k], self.got.at[slot], b + 4 + k, b + slot, plane_dev(owner)
                        ),
                    )

        def wait(self):
            for slot in range(2):
                rcopy(self.got.at[slot], self.got.at[slot], self.base, self.base + slot, sibling).wait_recv()

        def finish(self, put):
            self.wait()

            def body(own, one, two):
                loads = [lcopy(self.block(z), own), lcopy(self.got.at[0], one), lcopy(self.got.at[1], two)]
                for load in loads:
                    load.wait()
                for k in range(self.height // shard):
                    span = pl.ds(k * shard, shard)
                    put(k, own[span, :].astype(F32) + one[span, :].astype(F32) + two[span, :].astype(F32))

            shape = (self.height, self.grads.shape[1])
            pl.run_scoped(body, *[VM(shape, BF)] * 3)

    zg_o, zg_qkv = ZGather(r.w_o, shard), ZGather(r.w_qkv, KB, 2)
    sp_qkv = Spread(r.st_qkv)
    parts = range(len(PARTS))
    w_f, st_f = [r.w_f0, r.w_f1], [r.st_f0, r.st_f1]
    zg_f, sp_f = [ZGather(w, KB) for w in w_f], [Spread(st) for st in st_f]
    ag_normed, ag_cot, ag_two, ag_one = Gather(r.a_normed), Gather(r.a_cot), Gather(r.a_two), Gather(r.a_one)

    def mine_rows(whole, height):
        return whole.at[pl.ds(aligned((z * PL + q) * height, 16), height)]

    zg_o.start(r.in_o)
    local_o = lcopy(r.in_o, zg_o.block(z))
    base_small = slots(PL)
    for i in range(1, PL):
        copy = rcopy(r.in_small, r.small.at[z * PL + q], base_small + i, base_small + i, mate(i))
        copy.start()
        drains.append(copy.wait_send)
    local_small = lcopy(r.in_small, r.small.at[z * PL + q])
    def stage_qkv(v):
        lcopy(r.in_qkv, v).wait()
        for other in range(PL):
            for j in range(3):
                for zh in range(R):
                    at = j * D + zh * PL * HD + other * HD
                    r.st_qkv[other, :, j * QW + zh * HD : j * QW + (zh + 1) * HD] = v[:, at : at + HD]

    pl.run_scoped(stage_qkv, VM(r.in_qkv.shape, BF))
    sp_qkv.start(mine_rows(r.w_qkv, shard))
    local_qkv = lcopy(r.st_qkv.at[q], mine_rows(r.w_qkv, shard))
    local_f = [None] * len(PARTS)

    def stage_f(*bufs):
        loads = [lcopy(source, buf) for source, buf in zip((r.in_gate, r.in_up, r.in_down), bufs)]
        for load in loads:
            load.wait()
        for p, width in enumerate(PARTS):
            for other in range(PL):
                at = other * FW + STARTS[p]
                for k, source in enumerate(bufs):
                    st_f[p][other, :, k * width : (k + 1) * width] = source[:, at : at + width]
                if WC[p] > 3 * width:
                    st_f[p][other, :, 3 * width :] = jnp.zeros((shard, WC[p] - 3 * width), BF)

    def spread_f(p):
        sp_f[p].start(mine_rows(w_f[p], shard))
        local_f[p] = lcopy(st_f[p].at[q], mine_rows(w_f[p], shard))

    def arrived(spread, whole):
        spread.wait(lambda s: whole.at[pl.ds(aligned((z * PL + s) * shard, 16), shard)])

    pl.run_scoped(stage_f, *[VM(r.in_gate.shape, BF)] * 3)
    spread_f(0)

    local_small.wait()
    for i in range(1, PL):
        rcopy(r.in_small, r.small.at[z * PL + lax.rem(q - i + PL, PL)], base_small, base_small + i, mate(i)).wait_recv()
    base_smallz = slots(R)
    plane_small = r.small.at[pl.ds(z * PL, PL)]
    for i in range(1, R):
        copy = rcopy(plane_small, plane_small, base_smallz + i, base_smallz + i, plane_dev(lax.rem(z + i, R)))
        copy.start()
        drains.append(copy.wait_send)
    loads["tokens"].wait()
    loads["cot"].wait()
    tokens = r.v_tokens[...].astype(F32)
    unit, _ = norm_stats(tokens)
    for i in range(1, R):
        block = r.small.at[pl.ds(lax.rem(z - i + R, R) * PL, PL)]
        rcopy(block, block, base_smallz, base_smallz + i, sibling).wait_recv()
    for d in range(R * PL):
        for k in range(4):
            r.vec[k : k + 1, shard * d : shard * (d + 1)] = r.small[d, k : k + 1, 0:shard]
        for k in range(3):
            r.biases[3 * d + k : 3 * d + k + 1, 0:HD] = r.small[d, 4 + k : 5 + k, 0:HD]
    for j in range(3):
        for zh in range(R):
            row = r.biases[pl.ds(j * H + zh * PL + q, 1), 0:HD]
            r.bias[0:1, j * QW + zh * HD : j * QW + (zh + 1) * HD] = row
    r.x_normed[...] = (unit * r.vec[0:1, :] + r.vec[1:2, :]).astype(BF)
    ag_normed.start(r.x_normed)

    spread_f(1)
    ag_cot.start(r.v_cot)
    local_qkv.wait()
    arrived(sp_qkv, r.w_qkv)
    zg_qkv.start()
    local_f[0].wait()
    arrived(sp_f[0], w_f[0])
    zg_qkv.relay(0)
    zg_qkv.relay(1)
    zg_o.relay()
    zg_f[0].start()
    ag_normed.relay()
    ag_normed.wait()
    zg_qkv.wait()

    def lower(shape):
        return lax.rem(lax.broadcasted_iota(jnp.int32, shape, 1), HD) < ROT // 2

    def in_turn(shape):
        return lax.rem(lax.broadcasted_iota(jnp.int32, shape, 1), HD) < ROT

    TM = HS // 2
    local_tables.wait()

    @pl.loop(0, TOK // HS)
    def _(i):
        span = pl.ds(aligned(i * HS, HS), HS)
        projected = nn(r.a_normed[span, :], r.w_qkv[...]) + r.bias[0:1, :]
        for piece in range(2 * QW // 128):
            part = projected[:, piece * 128 : (piece + 1) * 128]
            other = jnp.where(lower(part.shape), pltpu.roll(part, 128 - ROT // 2, 1), pltpu.roll(part, ROT // 2, 1))
            turned = part * r.turns[0] + other * r.turns[1]
            r.qkv[span, piece * 128 : (piece + 1) * 128] = turned.astype(BF)
        r.qkv[span, 2 * QW :] = projected[:, 2 * QW :].astype(BF)

    heads = QW // HD

    def softmax_block(queries, keys, first):
        scores = nt(keys, queries) * 0.125
        at_key = lax.broadcasted_iota(jnp.int32, scores.shape, 0)
        at_query = lax.broadcasted_iota(jnp.int32, scores.shape, 1) + first
        allowed = at_key <= at_query
        scores = jnp.where(allowed, scores, -1e30)
        largest = jnp.max(scores, axis=0, keepdims=True)
        weights = jnp.where(allowed, jnp.exp(scores - largest), 0.0)
        return weights / jnp.sum(weights, axis=0, keepdims=True)

    QB = HS // 2

    @pl.loop(0, TOK // HS)
    def _(i):
        first = i * HS
        for h in range(heads):
            at = h * HD
            for blk in range(HS // QB):
                here = pl.ds(aligned(first + blk * QB, 16), QB)
                seen = pl.ds(aligned(first, 16), (blk + 1) * QB)
                probs = softmax_block(r.qkv[here, at : at + HD], r.qkv[seen, QW + at : QW + at + HD], blk * QB)
                out = tn(probs.astype(BF), r.qkv[seen, 2 * QW + at : 2 * QW + at + HD])
                r.att[here, at : at + HD] = out.astype(BF)

    local_f[1].wait()
    arrived(sp_f[1], w_f[1])
    ag_cot.relay()
    local_o.wait()
    zg_o.wait()

    red_att = Reduce(0)
    red_att.run([(r.att, r.w_o)], lambda x, w: nn(x, w[...]))
    zg_f[0].relay()
    zg_f[1].start()
    ag_cot.wait()
    middle = r.v_tokens[...].astype(F32) + red_att.finish()
    r.middle[...] = middle
    unit, _ = norm_stats(middle)
    r.x_two[...] = (unit * r.vec[2:3, :] + r.vec[3:4, :]).astype(BF)
    ag_two.start(r.x_two)

    hid, gug, g_f = [r.hid0, r.hid1], [r.gug0, r.gug1], [r.g_f0, r.g_f1]

    def feed_forward(p, then=None):
        width = PARTS[p]
        def body(w, *others):
            loads = []
            for load_in, buf in zip(earlier, others):
                loads.append(lcopy(load_in, buf))
            for s in range(R):
                zg_f[p].wait_block(s)
                loads.append(lcopy(zg_f[p].block(s), w.at[pl.ds(s * KB, KB)]))
            for load in loads:
                load.wait()

            def use(span):
                both = nn(r.a_two[span, :], w[:, : 2 * width])
                gate = both[:, :width]
                up = both[:, width:]
                sig = 1.0 / (1.0 + jnp.exp(-gate))
                swish = gate * sig
                hid[p][span, :] = (swish * up).astype(BF)
                hidden_grad = nn(r.a_cot[span, :], w[:, 2 * width : 3 * width])
                gug[p][span, :width] = (hidden_grad * up * sig * (1.0 + gate * (1.0 - sig))).astype(BF)
                gug[p][span, width:] = (hidden_grad * swish).astype(BF)

            if p == 0:
                ag_two.each(lambda s: use(pl.ds(aligned(s * rows, 16), rows)))
            else:

                @pl.loop(0, TOK // TM)
                def _(i):
                    use(pl.ds(aligned(i * TM, TM), TM))

            if then is not None:
                then(w, *others)

        earlier = [w_f[k].at[:, pl.ds(0, 2 * PARTS[k])] for k in range(p)]
        pl.run_scoped(body, VM(w_f[p].shape, BF), *[VM(ref.shape, BF) for ref in earlier])

    def grads_by_owner(terms, out, reduce, padded=None, steps=range(R)):
        width = out.shape[1]

        def body(tile, sem):
            pending = []

            def hand_on():
                store, step = pending.pop(0)
                store.wait()
                reduce.start_step(step)

            for step in steps:
                owner = R - 1 - step
                for at in range(1, R):
                    owner = jnp.where(z == at, ORDER[at][step], owner)
                for left, right, first in terms:
                    part = tn(left[:, pl.ds(aligned(owner * KB, KB), KB)], right[...])
                    tile[step % depth, :, first : first + right.shape[1]] = part.astype(BF)
                if padded is not None:
                    tile[step % depth, :, padded:] = jnp.zeros((KB, width - padded), BF)
                store = pltpu.make_async_copy(tile.at[step % depth], reduce.block(owner), sem.at[step % depth])
                store.start()
                pending.append((store, step))
                while len(pending) > (0 if step in (0, steps[-1]) else 1):
                    hand_on()

        depth = min(2, len(steps))
        pl.run_scoped(body, VM((depth, KB, width), BF), pltpu.SemaphoreType.DMA((depth,)))

    def feed_weight_grads(p, steps=range(R)):
        width = PARTS[p]
        terms = [(r.a_two, gug[p], 0), (r.a_cot, hid[p], 2 * width)]
        grads_by_owner(terms, g_f[p], zr_f[p], 3 * width if WC[p] > 3 * width else None, steps)

    zr_f = [ZReduce(r.g_f0, r.zin_f0, r.zx_f0, r.zs_f0, KB), ZReduce(r.g_f1, r.zin_f1, r.zx_f1, r.zs_f1, KB)]
    zr_o = ZReduce(r.g_o, r.zin_o, r.zx_o, r.zs_o, shard)
    zr_qkv = ZReduce(r.g_qkv, r.zin_qkv, r.zx_qkv, r.zs_qkv, KB)

    feed_forward(0)
    zg_f[1].relay()
    feed_weight_grads(0)
    red_two = Reduce(0, red_att)

    def back_into_layer(w_last, w_first):
        feed_weight_grads(1, (0,))
        weights = (w_first, w_last.at[:, pl.ds(0, 2 * PARTS[1])])
        red_two.run(list(zip(gug, weights)), lambda x, w: nt(x, w[...]))

    feed_forward(1, back_into_layer)
    feed_weight_grads(1, (1, 2, 3))
    zr_f[0].merge()
    two_grad = red_two.finish()
    unit, scale = norm_stats(r.middle[...])
    middle_grad = r.v_cot[...].astype(F32) + norm_back(two_grad, unit, scale, r.vec[2:3, :])
    r.middle_grad[...] = middle_grad
    ag_normed.drain()
    r.x_normed[...] = middle_grad.astype(BF)
    ag_one.start(r.x_normed)
    r.vec[6:7, :] = jnp.sum(two_grad * unit, axis=0, keepdims=True)
    r.vec[7:8, :] = jnp.sum(two_grad, axis=0, keepdims=True)

    red_mixed = Reduce(1)
    mixed_pairs = [(hid[p], (w_f[p].at[:, pl.ds(2 * PARTS[p], WC[p] - 2 * PARTS[p])],)) for p in parts]
    red_mixed.run(mixed_pairs, lambda x, w: nt(x, w[:, : x.shape[1]]), later=True)

    def att_grad(s):
        span = pl.ds(aligned(s * rows, 16), rows)
        pltpu.sync_copy(ag_one.block(s), r.a_two.at[span])
        r.a_cot[span, 0:QW] = nt(r.a_two[span, :], r.w_o[...]).astype(BF)

    ag_two.drain()
    ag_cot.drain()
    ag_one.each(att_grad)
    red_mixed.pass_on()
    def o_grad(buf):
        for k in range(R):
            span = pl.ds(k * KB, KB)
            buf[:, span] = tn(r.att[...], r.a_two[:, span]).astype(BF)
        pltpu.sync_copy(buf, r.g_o)

    pl.run_scoped(o_grad, VM((QW, D), BF))
    zr_o.start()
    zr_f[1].merge((0,))

    def attention_back(turn):
        @pl.loop(0, TOK // HS)
        def _(i):
            first = i * HS
            for h in range(heads):
                at = h * HD
                key_grad = [jnp.zeros((QB, HD), F32) for _ in range(HS // QB)]
                value_grad = [jnp.zeros((QB, HD), F32) for _ in range(HS // QB)]
                for blk in range(HS // QB):
                    here = pl.ds(aligned(first + blk * QB, 16), QB)
                    seen = pl.ds(aligned(first, 16), (blk + 1) * QB)
                    queries = r.qkv[here, at : at + HD]
                    keys = r.qkv[seen, QW + at : QW + at + HD]
                    values = r.qkv[seen, 2 * QW + at : 2 * QW + at + HD]
                    grads = r.a_cot[here, at : at + HD]
                    probs = softmax_block(queries, keys, blk * QB)
                    prob_grad = nt(values, grads)
                    delta = jnp.sum(probs * prob_grad, axis=0, keepdims=True)
                    score_grad = (probs * (prob_grad - delta)).astype(BF)
                    low_probs = probs.astype(BF)
                    turn[blk * QB : (blk + 1) * QB, at : at + HD] = tn(score_grad, keys) * 0.125
                    key_part = nn(score_grad, queries) * 0.125
                    value_part = nn(low_probs, grads)
                    for k in range(blk + 1):
                        key_grad[k] = key_grad[k] + key_part[k * QB : (k + 1) * QB]
                        value_grad[k] = value_grad[k] + value_part[k * QB : (k + 1) * QB]
                for k in range(HS // QB):
                    turn[k * QB : (k + 1) * QB, QW + at : QW + at + HD] = key_grad[k]
                    r.qkv[pl.ds(aligned(first + k * QB, 16), QB), 2 * QW + at : 2 * QW + at + HD] = value_grad[k].astype(BF)
            for piece in range(2 * QW // 128):
                part = turn[:, piece * 128 : (piece + 1) * 128]
                cross = part * r.turns[1]
                other = jnp.where(lower(part.shape), pltpu.roll(cross, 128 - ROT // 2, 1), pltpu.roll(cross, ROT // 2, 1))
                back = part * r.turns[0] + jnp.where(in_turn(part.shape), other, 0.0)
                r.qkv[pl.ds(aligned(first, 16), HS), piece * 128 : (piece + 1) * 128] = back.astype(BF)

    pl.run_scoped(attention_back, VM((HS, 2 * QW), F32))
    grads_by_owner([(r.a_normed, r.qkv, 0)], r.g_qkv, zr_qkv)
    zr_f[1].merge((1,))
    red_one = Reduce(0, red_two)
    red_one.run([(r.qkv, r.w_qkv)], lambda x, w: nt(x, w[...]))
    r.bias[0:1, :] = jnp.sum(r.qkv[...].astype(F32), axis=0, keepdims=True)

    zr_o.merge()
    back_f, back_qkv = [Spread(st) for st in st_f], Spread(r.st_qkv)
    pin_f = [r.pin_f0, r.pin_f1]

    def z_sum(reduce, sent, stage, spread, got):
        sent.wait_send()

        def put(k, total):
            stage[k] = total.astype(BF)

        reduce.finish(put)
        spread.start(got.at[q])
        return lcopy(stage.at[q], got.at[q])

    def pin_block(got):
        return lambda s: got.at[s]

    local_f[0] = z_sum(zr_f[0], sp_f[0], st_f[0], back_f[0], pin_f[0])
    zr_qkv.merge((0,))
    mixed = r.middle[...] + red_mixed.finish()
    r.x_two[...] = mixed.astype(BF)
    outputs = [lcopy(r.x_two, r.out_mixed)]
    zr_qkv.merge((1,))
    local_f[1] = z_sum(zr_f[1], sp_f[1], st_f[1], back_f[1], pin_f[1])
    one_grad = red_one.finish()
    unit, scale = norm_stats(r.v_tokens[...].astype(F32))
    r.middle_grad[...] = r.middle_grad[...] + norm_back(one_grad, unit, scale, r.vec[0:1, :])
    outputs.append(lcopy(r.middle_grad, r.out_tokens))
    r.vec[4:5, :] = jnp.sum(one_grad * unit, axis=0, keepdims=True)
    r.vec[5:6, :] = jnp.sum(one_grad, axis=0, keepdims=True)
    r.sg[...] = jnp.zeros_like(r.sg)
    for d in range(R * PL):
        for k in range(4):
            r.sg[d % PL, d // PL, k : k + 1, 0:shard] = r.vec[4 + k : 5 + k, shard * d : shard * (d + 1)]
    for j in range(3):
        for zh in range(R):
            g = j * H + zh * PL + q
            piece = r.bias[0:1, j * QW + zh * HD : j * QW + (zh + 1) * HD]
            r.sg[lax.rem(g // 3, PL), g // (3 * PL), pl.ds(4 + lax.rem(g, 3), 1), 0:HD] = piece
    base_sgp = slots(PL)
    for i in range(1, PL):
        other = lax.rem(q + i, PL)
        copy = rcopy(r.sg.at[other], r.sgp.at[i - 1], base_sgp + i, base_sgp + i, mate(i))
        copy.start()
        drains.append(copy.wait_send)
    zr_o.wait()
    outputs.append(lcopy(zr_o.block(z), r.own_o))
    local_f[0].wait()
    back_f[0].wait(pin_block(pin_f[0]))
    total = r.sg[q]
    for i in range(1, PL):
        rcopy(r.sgp.at[i - 1], r.sgp.at[i - 1], base_sgp, base_sgp + i, sibling).wait_recv()
        total = total + r.sgp[i - 1]
    r.sgs[...] = total
    base_sgz = slots(R)
    for i in range(1, R):
        t = lax.rem(z + i, R)
        copy = rcopy(r.sgs.at[t], r.sgz.at[i - 1], base_sgz + i, base_sgz + i, plane_dev(t))
        copy.start()
        drains.append(copy.wait_send)
    local_qkv = z_sum(zr_qkv, sp_qkv, r.st_qkv, back_qkv, r.pin_qkv)
    for i in range(1, R):
        rcopy(r.sgz.at[i - 1], r.sgz.at[i - 1], base_sgz, base_sgz + i, sibling).wait_recv()
    r.sgt[...] = r.sgs[z] + r.sgz[0] + r.sgz[1] + r.sgz[2]
    outputs.append(lcopy(r.sgt, r.out_small))
    local_f[1].wait()
    back_f[1].wait(pin_block(pin_f[1]))
    local_qkv.wait()
    back_qkv.wait(pin_block(r.pin_qkv))
    for copy in outputs:
        copy.wait()
    for spread in back_f:
        spread.wait_send()
    back_qkv.wait_send()
    ag_one.drain()
    red_mixed.drain()
    red_one.drain()
    for drain in drains:
        drain()
    assert counter[0] <= REMOTE_SEMS and local_count[0] <= LOCAL_SEMS, (counter, local_count)


def finish_outputs(got, parts, starts, planes, members, rows, shard, q_width, f_width):
    steps = 4
    tall, low = rows // steps, shard // steps

    def body(mixed_in, tokens_in, small_in, pin_qkv, own_o, zin_o, pin_f0, pin_f1, mixed, tokens, gains, bias, qkv, o, gate, up, down):
        mixed[0] = mixed_in[...]
        tokens[0] = tokens_in[...]
        o[...] = own_o[...].astype(F32) + zin_o[0].astype(F32) + zin_o[1].astype(F32)
        for k in range(4):
            gains[0:1, k * shard : (k + 1) * shard] = small_in[k : k + 1, 0:shard]
        for k in range(3):
            bias[0:1, k * HD : (k + 1) * HD] = small_in[4 + k : 5 + k, 0:HD]
        for other in range(members):
            for j in range(3):
                for zh in range(planes):
                    at = j * D + zh * members * HD + other * HD
                    qkv[:, at : at + HD] = pin_qkv[other, :, j * q_width + zh * HD : j * q_width + (zh + 1) * HD].astype(F32)
            for pin, width, start in zip((pin_f0, pin_f1), parts, starts):
                at = other * f_width + start
                for k, target in enumerate((gate, up, down)):
                    target[:, at : at + width] = pin[other, :, k * width : (k + 1) * width].astype(F32)

    def tiles(shape, axis, size):
        block = tuple(size if k == axis else n for k, n in enumerate(shape))
        return pl.BlockSpec(block, lambda i: tuple(i if k == axis else 0 for k in range(len(shape))))

    ins = [
        (got["out_mixed"], 0, tall), (got["out_tokens"], 0, tall), (got["out_small"], None, 0), (got["pin_qkv"], 1, low),
        (got["own_o"], 0, low), (got["zin_o"], 1, low), (got["pin_f0"], 1, low), (got["pin_f1"], 1, low),
    ]
    outs = dict(
        mixed=((1, rows, D), BF, 1, tall), tokens=((1, rows, D), F32, 1, tall),
        gains=((1, 4 * shard), F32, None, 0), bias=((1, 3 * HD), F32, None, 0),
        qkv=((shard, 3 * D), F32, 0, low), o=((shard, D), F32, 0, low),
        gate=((shard, FF), F32, 0, low), up=((shard, FF), F32, 0, low), down=((shard, FF), F32, 0, low),
    )
    results = pl.pallas_call(
        body,
        grid=(steps,),
        out_shape=[jax.ShapeDtypeStruct(shape, kind) for shape, kind, _, _ in outs.values()],
        in_specs=[tiles(array.shape, axis, size) for array, axis, size in ins],
        out_specs=[tiles(shape, axis, size) for shape, _, axis, size in outs.values()],
        name="finish",
    )(*[array for array, _, _ in ins])
    return dict(zip(outs, results))


def fast_local(tokens, out_grad, ln1_gain, ln1_shift, qkv_weight, qkv_bias, out_weight, ln2_gain, ln2_shift, gate_weight, up_weight, down_weight):
    planes, columns = lax.axis_size("batch") // 2, lax.axis_size("ctx")
    members = 2 * columns
    rows = tokens.shape[1]
    seq = rows * columns
    total = members * rows
    shard = qkv_weight.shape[0]
    q_width = D // members
    f_width = FF // members
    plane_rows = members * shard
    parts = (384, f_width - 384)
    dims = (planes, columns, members, rows, shard, q_width, f_width, parts)
    pieces = jnp.concatenate(
        [jnp.stack([ln1_gain, ln1_shift, ln2_gain, ln2_shift]), qkv_bias.reshape(3, HD)], axis=0
    ).astype(F32)
    small = jnp.pad(pieces, ((0, 1), (0, 128 - HD)))
    inputs = dict(
        in_tokens=(tokens.reshape(rows, D), ANY),
        in_cot=(out_grad.reshape(rows, D), ANY),
        in_small=(small, VM),
        in_qkv=(qkv_weight, ANY),
        in_o=(out_weight, ANY),
        in_gate=(gate_weight, ANY),
        in_up=(up_weight, ANY),
        in_down=(down_weight, ANY),
        tables=(jnp.asarray(turn_tables(seq)), ANY),
    )
    columns_f = [feed_columns(width) for width in parts]
    outs = dict(
        out_mixed=((rows, D), BF, ANY),
        out_tokens=((rows, D), F32, ANY),
        out_small=((8, 128), F32, ANY),
        pin_qkv=((members, shard, 3 * q_width), BF, ANY),
        own_o=((shard, D), BF, ANY),
        zin_o=((2, shard, D), BF, ANY),
    )
    for p, width in enumerate(columns_f):
        outs[f"pin_f{p}"] = ((members, shard, width), BF, ANY)
    final = list(outs)
    spaces = dict(
        a_one=(total, D),
        g_qkv=(D, 3 * q_width), g_o=(q_width, D),
        zin_qkv=(2, plane_rows, 3 * q_width),
        zx_qkv=(2, plane_rows, 3 * q_width), zx_o=(2, shard, D),
        zs_qkv=(2, plane_rows, 3 * q_width), zs_o=(2, shard, D),
    )
    for p, width in enumerate(columns_f):
        spaces[f"w_f{p}"] = spaces[f"g_f{p}"] = (D, width)
        for kind in ("zin", "zx", "zs"):
            spaces[f"{kind}_f{p}"] = (2, plane_rows, width)
    for name, shape in spaces.items():
        outs[name] = (shape, BF, ANY)
    scratch = dict(
        v_tokens=VM((rows, D), BF), v_cot=VM((rows, D), BF),
        turns=VM((2, seq, 128), F32),
        a_normed=VM((total, D), BF), a_two=VM((total, D), BF), a_cot=VM((total, D), BF),
        w_qkv=VM((D, 3 * q_width), BF), w_o=VM((q_width, D), BF),
        qkv=VM((total, 3 * q_width), BF), att=VM((total, q_width), BF),
        st_qkv=VM((members, shard, 3 * q_width), BF),
        small=VM((planes * members, 8, 128), F32), sg=VM((members, planes, 8, 128), F32),
        sgz=VM((planes - 1, 8, 128), F32), sgs=VM((planes, 8, 128), F32), sgp=VM((members - 1, planes, 8, 128), F32), sgt=VM((8, 128), F32),
        vec=VM((8, D), F32), biases=VM((3 * H, 128), F32), bias=VM((8, 3 * q_width), F32),
        x_normed=VM((rows, D), BF), x_two=VM((rows, D), BF),
        middle=VM((rows, D), F32), middle_grad=VM((rows, D), F32),
        mine=VM((seq, D), BF),
    )
    for p, width in enumerate(parts):
        scratch[f"st_f{p}"] = VM((members, shard, columns_f[p]), BF)
        scratch[f"hid{p}"], scratch[f"gug{p}"] = VM((total, width), BF), VM((total, 2 * width), BF)
    for k in range(2):
        scratch[f"sibout{k}"] = VM((seq, D), BF)
        scratch[f"theirs{k}"] = VM((seq, D), BF)
        scratch[f"redout{k}"] = VM((columns - 1, rows, D), BF)
        scratch[f"redin{k}"] = VM((columns - 1, rows, D), BF)
        scratch[f"redown{k}"] = VM((rows, D), F32 if k == 0 else BF)
    scratch["ss"] = pltpu.SemaphoreType.DMA((REMOTE_SEMS,))
    scratch["rs"] = pltpu.SemaphoreType.DMA((REMOTE_SEMS,))
    scratch["ls"] = pltpu.SemaphoreType.DMA((LOCAL_SEMS,))
    results = pl.pallas_call(
        functools.partial(layer_kernel, dims, list(inputs), list(outs), list(scratch)),
        out_shape=[jax.ShapeDtypeStruct(shape, kind) for shape, kind, _ in outs.values()],
        in_specs=[pl.BlockSpec(memory_space=place) for _, place in inputs.values()],
        out_specs=[pl.BlockSpec(memory_space=place) for _, _, place in outs.values()],
        scratch_shapes=list(scratch.values()),
        compiler_params=pltpu.CompilerParams(collective_id=0, has_side_effects=True, vmem_limit_bytes=63 * 2**20),
        cost_estimate=pl.CostEstimate(flops=42 * 10**9, bytes_accessed=300 * 10**6, transcendentals=0),
        name="layer",
    )(*[array for array, _ in inputs.values()])
    got = dict(zip(final, results))
    f_starts = [sum(parts[:p]) for p in range(len(parts))]
    done = finish_outputs(got, parts, f_starts, planes, members, rows, shard, q_width, f_width)
    return (
        done["mixed"],
        done["tokens"],
        done["gains"].reshape(4, shard)[0],
        done["gains"].reshape(4, shard)[1],
        done["qkv"],
        done["bias"].reshape(3 * HD),
        done["o"],
        done["gains"].reshape(4, shard)[2],
        done["gains"].reshape(4, shard)[3],
        done["gate"],
        done["up"],
        done["down"],
    )


def fits(mesh):
    return mesh.shape["batch"] == 8 and mesh.shape["ctx"] == 4


def solution(mesh):
    in_specs = (
        P("batch", "ctx", None),
        P("batch", "ctx", None),
        P(("batch", "ctx")),
        P(("batch", "ctx")),
        P(("batch", "ctx"), None),
        P(("batch", "ctx")),
        P(("batch", "ctx"), None),
        P(("batch", "ctx")),
        P(("batch", "ctx")),
        P(("batch", "ctx"), None),
        P(("batch", "ctx"), None),
        P(("batch", "ctx"), None),
    )
    out_specs = (
        P("batch", "ctx", None),
        P("batch", "ctx", None),
        P(("batch", "ctx")),
        P(("batch", "ctx")),
        P(("batch", "ctx"), None),
        P(("batch", "ctx")),
        P(("batch", "ctx"), None),
        P(("batch", "ctx")),
        P(("batch", "ctx")),
        P(("batch", "ctx"), None),
        P(("batch", "ctx"), None),
        P(("batch", "ctx"), None),
    )
    body = fast_local if fits(mesh) else local
    return jax.shard_map(body, mesh=mesh, in_specs=in_specs, out_specs=out_specs, check_vma=False)
```

profile of v0, /device:TPU:0, one launch (start us, length us, event | category | flops | bytes accessed | tf_op | source)
XLA Modules:
  0.0 437.9 jit_solution(18185399633992727118)
XLA Ops:
  0.6 0.7 reshape.50
  1.4 0.7 concatenate.3
  2.1 0.6 pad_convert_fusion.refs_2_
  2.7 427.2 %layer.1 = (bf16[128,2048]{1,0:T(8,128)(2,1)}, f32[128,2048]{1,0:T(8,128)}, f32[8,128]{1,0:T(8,128)}, bf16[8,64,768]{2,1,0:T(8,128)(2,1)}, bf16[64,2048]{1,0:T(8...) custom-call(bf16[128,2048]{1,0:T(8,128)(2,1)} %bitcast.19, ...), custom_call_target="tpu_custom_call" | custom-call | flops 41999998976 | bytes 300000000 | tf_op jit(solution)/shard_map/layer/pallas_call | solution.py:1279
  429.9 6.2 %finish.1 = (bf16[1,128,2048]{2,1,0:T(8,128)(2,1)}, f32[1,128,2048]{2,1,0:T(8,128)}, f32[1,256]{1,0:T(1,128)}, f32[1,192]{1,0:T(1,128)}, f32[64,6144]{1,0:T(8,12...) custom-call(bf16[128,2048]{1,0:T(8,128)(2,1)} %get-tuple-element.29.mixed_in, ...), custom_call_target="tpu_custom_call" | custom-call | tf_op jit(solution)/shard_map/finish/pallas_call | solution.py:1190
  436.1 1.3 slice_bitcast_fusion
where the time goes:
time: 445 us; the launch traced here: 438 us
  Pallas kernels  433 us (97%)
    pallas_call x1, Pallas kernels, fast_local(): pl.pallas_call(functools.partial(layer_kernel, dims, list(inputs), list(o...  427 us

commit v1 on v0

--- a/solution.py
+++ b/solution.py
@@ -295,7 +295,7 @@
 MESH = pl.DeviceIdType.MESH
 ANY = pl.ANY
 VM = pltpu.VMEM
-REMOTE_SEMS = 240
+REMOTE_SEMS = 320
 LOCAL_SEMS = 64
 
 
@@ -347,6 +347,11 @@
 
 def feed_columns(width):
     return 2 * width + -(-width // 128) * 128
+
+
+def qkv_lane(kind, head, heads):
+    half = heads // 2
+    return ((head // half * 3 + kind) * half + head % half) * HD
 
 
 class Names:
@@ -368,6 +373,13 @@
     KB = PL * shard
     STARTS = [sum(PARTS[:p]) for p in range(len(PARTS))]
     WC = [feed_columns(width) for width in PARTS]
+    heads = QW // HD
+    QH = QW // 2
+
+    def lanes(kind, head):
+        first = qkv_lane(kind, head, heads)
+        return slice(first, first + HD)
+
 
     at_plane = [z == at for at in range(R)]
     counter = [0]
@@ -410,6 +422,12 @@
     loads = {name: lcopy(getattr(r, "in_" + name), getattr(r, "v_" + name)) for name in ("tokens", "cot")}
 
     local_tables = lcopy(r.tables, r.turns)
+    r.sgt[...] = jnp.zeros_like(r.sgt)
+    for k, vector in enumerate((r.in_g0, r.in_g1, r.in_g2, r.in_g3)):
+        r.sgt[k : k + 1, 0:shard] = vector[...].astype(F32)
+    for k in range(3):
+        r.sgt[4 + k : 5 + k, 0:HD] = r.in_bias[0:1, k * HD : (k + 1) * HD].astype(F32)
+
     barrier = pltpu.get_barrier_semaphore()
     for i in range(1, PL):
         pl.semaphore_signal(barrier, inc=1, device_id=mate(i), device_id_type=MESH)
@@ -555,10 +573,11 @@
                 self.wait_one(i)
             self.local.wait()
 
-        def each(self, use):
-            self.local.wait()
-
-            @pl.loop(0, C)
+        def each(self, use, first=0, last=None):
+            if first == 0:
+                self.local.wait()
+
+            @pl.loop(first, C if last is None else last)
             def _(i):
                 @pl.when(i > 0)
                 def _():
@@ -576,7 +595,7 @@
             self.before = before
 
 
-        def run(self, pairs, compute, later=False):
+        def run(self, pairs, compute, later=False, more=False, only_prepare=False):
             chunk_rows = HS // 2
 
             def to_sibling(chunk):
@@ -588,7 +607,10 @@
                 for (x, _), w in zip(pairs, weights):
                     term = compute(x[pl.ds(aligned(seq * HS + chunk * chunk_rows, 16), chunk_rows), :], w)
                     total = term if total is None else total + term
-                target[chunk * chunk_rows : (chunk + 1) * chunk_rows, :] = total.astype(BF)
+                span = pl.ds(chunk * chunk_rows, chunk_rows)
+                if more:
+                    total = total + target[span, :].astype(F32)
+                target[span, :] = total.astype(BF)
 
             def pass_on(chunk):
                 to_sibling(chunk).wait_recv()
@@ -617,8 +639,13 @@
                         weights.append(w)
                 for load in loads:
                     load.wait()
-                if self.before is not None:
+                if self.before is not None and not more:
                     self.before.drain()
+                if only_prepare:
+                    for chunk in range(2):
+                        product(self.sibout, weights, 1 - core, chunk)
+                        product(r.mine, weights, core, chunk)
+                    return
                 product(self.sibout, weights, 1 - core, 0)
                 to_sibling(0).start()
                 product(r.mine, weights, core, 0)
@@ -634,6 +661,9 @@
             self.drain = lambda: self.drain_all(to_sibling)
             self.pass_on = lambda: (pass_on(0), pass_on(1))
 
+        def prepare(self, pairs, compute):
+            self.run(pairs, compute, only_prepare=True)
+
         def to_row(self, i, blk):
             return rcopy(self.out.at[i - 1], self.got.at[i - 1], self.base + i, self.base + i, (batch, blk))
 
@@ -680,7 +710,7 @@
                 return
             if via is None:
                 slot = 1 if owner < at else 0
-                make = lambda: rcopy(self.block(owner), self.got.at[slot], b + 3, b + slot, plane_dev(owner))
+                return
             elif owner == via:
                 slot = 0 if at == 0 else 1
                 make = lambda: rcopy(self.block(owner), self.got.at[slot], b + 2, b + slot, plane_dev(via))
@@ -699,6 +729,12 @@
 
         def merge(self, steps=(0, 1)):
             b = self.base
+            if 0 in steps:
+                for at, owner, slot in ((1, 0, 1), (2, 3, 0)):
+                    self.guarded(
+                        at_plane[at],
+                        lambda owner=owner, slot=slot: rcopy(self.block(owner), self.got.at[slot], b + 3, b + slot, plane_dev(owner)),
+                    )
             for k in steps:
                 for at, to, slots_at in ((1, (3, 2), (1, 0)), (2, (0, 1), (0, 1))):
                     owner = to[k]
@@ -747,7 +783,10 @@
     zg_o, zg_qkv = ZGather(r.w_o, shard), ZGather(r.w_qkv, KB, 2)
     sp_qkv = Spread(r.st_qkv)
     parts = range(len(PARTS))
-    w_f, st_f = [r.w_f0, r.w_f1], [r.st_f0, r.st_f1]
+    def each_part(name):
+        return [getattr(r, f"{name}{p}") for p in parts]
+
+    w_f, st_f = each_part("w_f"), each_part("st_f")
     zg_f, sp_f = [ZGather(w, KB) for w in w_f], [Spread(st) for st in st_f]
     ag_normed, ag_cot, ag_two, ag_one = Gather(r.a_normed), Gather(r.a_cot), Gather(r.a_two), Gather(r.a_one)
 
@@ -757,18 +796,19 @@
     zg_o.start(r.in_o)
     local_o = lcopy(r.in_o, zg_o.block(z))
     base_small = slots(PL)
+    small_sent = []
     for i in range(1, PL):
-        copy = rcopy(r.in_small, r.small.at[z * PL + q], base_small + i, base_small + i, mate(i))
+        copy = rcopy(r.sgt, r.small.at[z * PL + q], base_small + i, base_small + i, mate(i))
         copy.start()
-        drains.append(copy.wait_send)
-    local_small = lcopy(r.in_small, r.small.at[z * PL + q])
+        small_sent.append(copy)
+    local_small = lcopy(r.sgt, r.small.at[z * PL + q])
     def stage_qkv(v):
         lcopy(r.in_qkv, v).wait()
         for other in range(PL):
             for j in range(3):
                 for zh in range(R):
                     at = j * D + zh * PL * HD + other * HD
-                    r.st_qkv[other, :, j * QW + zh * HD : j * QW + (zh + 1) * HD] = v[:, at : at + HD]
+                    r.st_qkv[other, :, lanes(j, zh)] = v[:, at : at + HD]
 
     pl.run_scoped(stage_qkv, VM(r.in_qkv.shape, BF))
     sp_qkv.start(mine_rows(r.w_qkv, shard))
@@ -799,7 +839,7 @@
 
     local_small.wait()
     for i in range(1, PL):
-        rcopy(r.in_small, r.small.at[z * PL + lax.rem(q - i + PL, PL)], base_small, base_small + i, mate(i)).wait_recv()
+        rcopy(r.sgt, r.small.at[z * PL + lax.rem(q - i + PL, PL)], base_small, base_small + i, mate(i)).wait_recv()
     base_smallz = slots(R)
     plane_small = r.small.at[pl.ds(z * PL, PL)]
     for i in range(1, R):
@@ -821,11 +861,12 @@
     for j in range(3):
         for zh in range(R):
             row = r.biases[pl.ds(j * H + zh * PL + q, 1), 0:HD]
-            r.bias[0:1, j * QW + zh * HD : j * QW + (zh + 1) * HD] = row
+            r.bias[0:1, lanes(j, zh)] = row
     r.x_normed[...] = (unit * r.vec[0:1, :] + r.vec[1:2, :]).astype(BF)
     ag_normed.start(r.x_normed)
 
     spread_f(1)
+    spread_f(2)
     ag_cot.start(r.v_cot)
     local_qkv.wait()
     arrived(sp_qkv, r.w_qkv)
@@ -853,14 +894,14 @@
     def _(i):
         span = pl.ds(aligned(i * HS, HS), HS)
         projected = nn(r.a_normed[span, :], r.w_qkv[...]) + r.bias[0:1, :]
-        for piece in range(2 * QW // 128):
-            part = projected[:, piece * 128 : (piece + 1) * 128]
+        for first in [half * 3 * QH + k * 128 for half in range(2) for k in range(2 * QH // 128)]:
+            part = projected[:, first : first + 128]
             other = jnp.where(lower(part.shape), pltpu.roll(part, 128 - ROT // 2, 1), pltpu.roll(part, ROT // 2, 1))
             turned = part * r.turns[0] + other * r.turns[1]
-            r.qkv[span, piece * 128 : (piece + 1) * 128] = turned.astype(BF)
-        r.qkv[span, 2 * QW :] = projected[:, 2 * QW :].astype(BF)
-
-    heads = QW // HD
+            r.qkv[span, first : first + 128] = turned.astype(BF)
+        for half in range(2):
+            values = slice(half * 3 * QH + 2 * QH, (half + 1) * 3 * QH)
+            r.qkv[span, values] = projected[:, values].astype(BF)
 
     def softmax_block(queries, keys, first):
         scores = nt(keys, queries) * 0.125
@@ -874,20 +915,21 @@
 
     QB = HS // 2
 
-    @pl.loop(0, TOK // HS)
-    def _(i):
-        first = i * HS
+    kept = []
+    for seq, keep in enumerate((r.sibout1, r.theirs1)):
+
         for h in range(heads):
-            at = h * HD
             for blk in range(HS // QB):
-                here = pl.ds(aligned(first + blk * QB, 16), QB)
-                seen = pl.ds(aligned(first, 16), (blk + 1) * QB)
-                probs = softmax_block(r.qkv[here, at : at + HD], r.qkv[seen, QW + at : QW + at + HD], blk * QB)
-                out = tn(probs.astype(BF), r.qkv[seen, 2 * QW + at : 2 * QW + at + HD])
-                r.att[here, at : at + HD] = out.astype(BF)
-
-    local_f[1].wait()
-    arrived(sp_f[1], w_f[1])
+                here = pl.ds(seq * HS + blk * QB, QB)
+                seen = pl.ds(seq * HS, (blk + 1) * QB)
+                probs = softmax_block(r.qkv[here, lanes(0, h)], r.qkv[seen, lanes(1, h)], blk * QB).astype(BF)
+                keep[0 : (blk + 1) * QB, h * HS + blk * QB : h * HS + (blk + 1) * QB] = probs
+                r.att[here, h * HD : (h + 1) * HD] = tn(probs, r.qkv[seen, lanes(2, h)]).astype(BF)
+        kept.append(lcopy(keep, r.probs.at[pl.ds(seq * HS, HS)]))
+
+    for p in (1, 2):
+        local_f[p].wait()
+        arrived(sp_f[p], w_f[p])
     ag_cot.relay()
     local_o.wait()
     zg_o.wait()
@@ -901,16 +943,18 @@
     r.middle[...] = middle
     unit, _ = norm_stats(middle)
     r.x_two[...] = (unit * r.vec[2:3, :] + r.vec[3:4, :]).astype(BF)
+    for copy in kept:
+        copy.wait()
     ag_two.start(r.x_two)
-
-    hid, gug, g_f = [r.hid0, r.hid1], [r.gug0, r.gug1], [r.g_f0, r.g_f1]
+    zg_f[1].relay()
+    zg_f[2].start()
+
+    hid, gug, g_f = each_part("hid"), each_part("gug"), each_part("g_f")
 
     def feed_forward(p, then=None):
         width = PARTS[p]
-        def body(w, *others):
+        def body(w):
             loads = []
-            for load_in, buf in zip(earlier, others):
-                loads.append(lcopy(load_in, buf))
             for s in range(R):
                 zg_f[p].wait_block(s)
                 loads.append(lcopy(zg_f[p].block(s), w.at[pl.ds(s * KB, KB)]))
@@ -937,10 +981,9 @@
                     use(pl.ds(aligned(i * TM, TM), TM))
 
             if then is not None:
-                then(w, *others)
-
-        earlier = [w_f[k].at[:, pl.ds(0, 2 * PARTS[k])] for k in range(p)]
-        pl.run_scoped(body, VM(w_f[p].shape, BF), *[VM(ref.shape, BF) for ref in earlier])
+                then(w)
+
+        pl.run_scoped(body, VM(w_f[p].shape, BF))
 
     def grads_by_owner(terms, out, reduce, padded=None, steps=range(R)):
         width = out.shape[1]
@@ -976,23 +1019,26 @@
         terms = [(r.a_two, gug[p], 0), (r.a_cot, hid[p], 2 * width)]
         grads_by_owner(terms, g_f[p], zr_f[p], 3 * width if WC[p] > 3 * width else None, steps)
 
-    zr_f = [ZReduce(r.g_f0, r.zin_f0, r.zx_f0, r.zs_f0, KB), ZReduce(r.g_f1, r.zin_f1, r.zx_f1, r.zs_f1, KB)]
+    zr_f = [ZReduce(*bufs, KB) for bufs in zip(g_f, each_part("zin_f"), each_part("zx_f"), each_part("zs_f"))]
     zr_o = ZReduce(r.g_o, r.zin_o, r.zx_o, r.zs_o, shard)
-    zr_qkv = ZReduce(r.g_qkv, r.zin_qkv, r.zx_qkv, r.zs_qkv, KB)
+    g_q = [r.g_q0, r.g_q1]
+    zr_q = [ZReduce(g_q[0], r.zin_q0, r.zx_q0, r.zs_q0, KB), ZReduce(g_q[1], r.zin_q1, r.zx_q1, r.zs_q1, KB)]
 
     feed_forward(0)
-    zg_f[1].relay()
+    zg_f[2].relay()
     feed_weight_grads(0)
+    feed_forward(1)
+    feed_weight_grads(1)
     red_two = Reduce(0, red_att)
-
-    def back_into_layer(w_last, w_first):
-        feed_weight_grads(1, (0,))
-        weights = (w_first, w_last.at[:, pl.ds(0, 2 * PARTS[1])])
-        red_two.run(list(zip(gug, weights)), lambda x, w: nt(x, w[...]))
-
-    feed_forward(1, back_into_layer)
-    feed_weight_grads(1, (1, 2, 3))
-    zr_f[0].merge()
+    first_pairs = [(gug[p], (w_f[p].at[:, pl.ds(0, 2 * PARTS[p])],)) for p in (0, 1)]
+    red_two.prepare(first_pairs, lambda x, w: nt(x, w[...]))
+
+    def back_into_layer(w):
+        feed_weight_grads(2, (0,))
+        red_two.run([(gug[2], w.at[:, pl.ds(0, 2 * PARTS[2])])], lambda x, w: nt(x, w[...]), more=True)
+
+    feed_forward(2, back_into_layer)
+    feed_weight_grads(2, (1, 2, 3))
     two_grad = red_two.finish()
     unit, scale = norm_stats(r.middle[...])
     middle_grad = r.v_cot[...].astype(F32) + norm_back(two_grad, unit, scale, r.vec[2:3, :])
@@ -1003,19 +1049,46 @@
     r.vec[6:7, :] = jnp.sum(two_grad * unit, axis=0, keepdims=True)
     r.vec[7:8, :] = jnp.sum(two_grad, axis=0, keepdims=True)
 
+    zr_f[0].merge()
     red_mixed = Reduce(1)
     mixed_pairs = [(hid[p], (w_f[p].at[:, pl.ds(2 * PARTS[p], WC[p] - 2 * PARTS[p])],)) for p in parts]
     red_mixed.run(mixed_pairs, lambda x, w: nt(x, w[:, : x.shape[1]]), later=True)
 
+    attg = gug[1]
+
     def att_grad(s):
         span = pl.ds(aligned(s * rows, 16), rows)
         pltpu.sync_copy(ag_one.block(s), r.a_two.at[span])
-        r.a_cot[span, 0:QW] = nt(r.a_two[span, :], r.w_o[...]).astype(BF)
+        attg[span, 0:QW] = nt(r.a_two[span, :], r.w_o[...]).astype(BF)
 
     ag_two.drain()
     ag_cot.drain()
-    ag_one.each(att_grad)
+    zr_f[1].merge()
+
+    weights_back = lcopy(r.probs, r.a_cot)
+
+    back_f, back_q = [Spread(st) for st in st_f], [Spread(r.st_q0), Spread(r.st_q1)]
+    pin_f = each_part("pin_f")
+    pin_q, st_q = [r.pin_q0, r.pin_q1], [r.st_q0, r.st_q1]
+
+    def pin_block(got):
+        return lambda s: got.at[s]
+
+    def z_sum(reduce, sent, stage, spread, got):
+        if sent is not None:
+            sent.wait_send()
+
+        def put(k, total):
+            stage[k] = total.astype(BF)
+
+        reduce.finish(put)
+        spread.start(got.at[q])
+        return lcopy(stage.at[q], got.at[q])
+
+    ag_one.each(att_grad, 0, C - 1)
+    local_f[0] = z_sum(zr_f[0], sp_f[0], st_f[0], back_f[0], pin_f[0])
     red_mixed.pass_on()
+    ag_one.each(att_grad, C - 1, C)
     def o_grad(buf):
         for k in range(R):
             span = pl.ds(k * KB, KB)
@@ -1024,75 +1097,63 @@
 
     pl.run_scoped(o_grad, VM((QW, D), BF))
     zr_o.start()
-    zr_f[1].merge((0,))
-
-    def attention_back(turn):
-        @pl.loop(0, TOK // HS)
-        def _(i):
-            first = i * HS
-            for h in range(heads):
-                at = h * HD
-                key_grad = [jnp.zeros((QB, HD), F32) for _ in range(HS // QB)]
-                value_grad = [jnp.zeros((QB, HD), F32) for _ in range(HS // QB)]
-                for blk in range(HS // QB):
-                    here = pl.ds(aligned(first + blk * QB, 16), QB)
-                    seen = pl.ds(aligned(first, 16), (blk + 1) * QB)
-                    queries = r.qkv[here, at : at + HD]
-                    keys = r.qkv[seen, QW + at : QW + at + HD]
-                    values = r.qkv[seen, 2 * QW + at : 2 * QW + at + HD]
-                    grads = r.a_cot[here, at : at + HD]
-                    probs = softmax_block(queries, keys, blk * QB)
-                    prob_grad = nt(values, grads)
-                    delta = jnp.sum(probs * prob_grad, axis=0, keepdims=True)
-                    score_grad = (probs * (prob_grad - delta)).astype(BF)
-                    low_probs = probs.astype(BF)
-                    turn[blk * QB : (blk + 1) * QB, at : at + HD] = tn(score_grad, keys) * 0.125
-                    key_part = nn(score_grad, queries) * 0.125
-                    value_part = nn(low_probs, grads)
-                    for k in range(blk + 1):
-                        key_grad[k] = key_grad[k] + key_part[k * QB : (k + 1) * QB]
-                        value_grad[k] = value_grad[k] + value_part[k * QB : (k + 1) * QB]
-                for k in range(HS // QB):
-                    turn[k * QB : (k + 1) * QB, QW + at : QW + at + HD] = key_grad[k]
-                    r.qkv[pl.ds(aligned(first + k * QB, 16), QB), 2 * QW + at : 2 * QW + at + HD] = value_grad[k].astype(BF)
-            for piece in range(2 * QW // 128):
-                part = turn[:, piece * 128 : (piece + 1) * 128]
-                cross = part * r.turns[1]
-                other = jnp.where(lower(part.shape), pltpu.roll(cross, 128 - ROT // 2, 1), pltpu.roll(cross, ROT // 2, 1))
-                back = part * r.turns[0] + jnp.where(in_turn(part.shape), other, 0.0)
-                r.qkv[pl.ds(aligned(first, 16), HS), piece * 128 : (piece + 1) * 128] = back.astype(BF)
-
-    pl.run_scoped(attention_back, VM((HS, 2 * QW), F32))
-    grads_by_owner([(r.a_normed, r.qkv, 0)], r.g_qkv, zr_qkv)
-    zr_f[1].merge((1,))
+    zr_f[2].merge((0,))
+
+    def attention_back(half):
+        def body(turn):
+            @pl.loop(0, TOK // HS)
+            def _(i):
+                first = i * HS
+                for hh in range(heads // 2):
+                    h = half * heads // 2 + hh
+                    key_grad = [jnp.zeros((QB, HD), F32) for _ in range(HS // QB)]
+                    value_grad = [jnp.zeros((QB, HD), F32) for _ in range(HS // QB)]
+                    for blk in range(HS // QB):
+                        here = pl.ds(aligned(first + blk * QB, 16), QB)
+                        seen = pl.ds(aligned(first, 16), (blk + 1) * QB)
+                        queries, keys, values = r.qkv[here, lanes(0, h)], r.qkv[seen, lanes(1, h)], r.qkv[seen, lanes(2, h)]
+                        grads = attg[here, h * HD : (h + 1) * HD]
+                        low_probs = r.a_cot[seen, h * HS + blk * QB : h * HS + (blk + 1) * QB]
+                        probs = low_probs.astype(F32)
+                        prob_grad = nt(values, grads)
+                        delta = jnp.sum(probs * prob_grad, axis=0, keepdims=True)
+                        score_grad = (probs * (prob_grad - delta)).astype(BF)
+                        turn[blk * QB : (blk + 1) * QB, hh * HD : (hh + 1) * HD] = tn(score_grad, keys) * 0.125
+                        key_part = nn(score_grad, queries) * 0.125
+                        value_part = nn(low_probs, grads)
+                        for k in range(blk + 1):
+                            key_grad[k] = key_grad[k] + key_part[k * QB : (k + 1) * QB]
+                            value_grad[k] = value_grad[k] + value_part[k * QB : (k + 1) * QB]
+                    for k in range(HS // QB):
+                        turn[k * QB : (k + 1) * QB, QH + hh * HD : QH + (hh + 1) * HD] = key_grad[k]
+                        r.qkv[pl.ds(aligned(first + k * QB, 16), QB), lanes(2, h)] = value_grad[k].astype(BF)
+                for k in range(2 * QH // 128):
+                    part = turn[:, k * 128 : (k + 1) * 128]
+                    cross = part * r.turns[1]
+                    other = jnp.where(lower(part.shape), pltpu.roll(cross, 128 - ROT // 2, 1), pltpu.roll(cross, ROT // 2, 1))
+                    back = part * r.turns[0] + jnp.where(in_turn(part.shape), other, 0.0)
+                    at = half * 3 * QH + k * 128
+                    r.qkv[pl.ds(aligned(first, 16), HS), at : at + 128] = back.astype(BF)
+
+        pl.run_scoped(body, VM((HS, 2 * QH), F32))
+        grads_by_owner([(r.a_normed, r.qkv.at[:, pl.ds(half * 3 * QH, 3 * QH)], 0)], g_q[half], zr_q[half])
+
+    weights_back.wait()
+    attention_back(0)
+    attention_back(1)
+    zr_f[2].merge((1,))
     red_one = Reduce(0, red_two)
     red_one.run([(r.qkv, r.w_qkv)], lambda x, w: nt(x, w[...]))
     r.bias[0:1, :] = jnp.sum(r.qkv[...].astype(F32), axis=0, keepdims=True)
 
     zr_o.merge()
-    back_f, back_qkv = [Spread(st) for st in st_f], Spread(r.st_qkv)
-    pin_f = [r.pin_f0, r.pin_f1]
-
-    def z_sum(reduce, sent, stage, spread, got):
-        sent.wait_send()
-
-        def put(k, total):
-            stage[k] = total.astype(BF)
-
-        reduce.finish(put)
-        spread.start(got.at[q])
-        return lcopy(stage.at[q], got.at[q])
-
-    def pin_block(got):
-        return lambda s: got.at[s]
-
-    local_f[0] = z_sum(zr_f[0], sp_f[0], st_f[0], back_f[0], pin_f[0])
-    zr_qkv.merge((0,))
+    local_f[1] = z_sum(zr_f[1], sp_f[1], st_f[1], back_f[1], pin_f[1])
+    zr_q[0].merge()
     mixed = r.middle[...] + red_mixed.finish()
     r.x_two[...] = mixed.astype(BF)
     outputs = [lcopy(r.x_two, r.out_mixed)]
-    zr_qkv.merge((1,))
-    local_f[1] = z_sum(zr_f[1], sp_f[1], st_f[1], back_f[1], pin_f[1])
+    local_f[2] = z_sum(zr_f[2], sp_f[2], st_f[2], back_f[2], pin_f[2])
+    zr_q[1].merge()
     one_grad = red_one.finish()
     unit, scale = norm_stats(r.v_tokens[...].astype(F32))
     r.middle_grad[...] = r.middle_grad[...] + norm_back(one_grad, unit, scale, r.vec[0:1, :])
@@ -1106,7 +1167,7 @@
     for j in range(3):
         for zh in range(R):
             g = j * H + zh * PL + q
-            piece = r.bias[0:1, j * QW + zh * HD : j * QW + (zh + 1) * HD]
+            piece = r.bias[0:1, lanes(j, zh)]
             r.sg[lax.rem(g // 3, PL), g // (3 * PL), pl.ds(4 + lax.rem(g, 3), 1), 0:HD] = piece
     base_sgp = slots(PL)
     for i in range(1, PL):
@@ -1129,20 +1190,26 @@
         copy = rcopy(r.sgs.at[t], r.sgz.at[i - 1], base_sgz + i, base_sgz + i, plane_dev(t))
         copy.start()
         drains.append(copy.wait_send)
-    local_qkv = z_sum(zr_qkv, sp_qkv, r.st_qkv, back_qkv, r.pin_qkv)
+    local_q = [z_sum(zr_q[half], None, st_q[half], back_q[half], pin_q[half]) for half in range(2)]
     for i in range(1, R):
         rcopy(r.sgz.at[i - 1], r.sgz.at[i - 1], base_sgz, base_sgz + i, sibling).wait_recv()
+    for copy in small_sent:
+        copy.wait_send()
     r.sgt[...] = r.sgs[z] + r.sgz[0] + r.sgz[1] + r.sgz[2]
     outputs.append(lcopy(r.sgt, r.out_small))
-    local_f[1].wait()
-    back_f[1].wait(pin_block(pin_f[1]))
-    local_qkv.wait()
-    back_qkv.wait(pin_block(r.pin_qkv))
+    for p in (1, 2):
+        local_f[p].wait()
+        back_f[p].wait(pin_block(pin_f[p]))
+    for half in range(2):
+        local_q[half].wait()
+        back_q[half].wait(pin_block(pin_q[half]))
     for copy in outputs:
         copy.wait()
     for spread in back_f:
         spread.wait_send()
-    back_qkv.wait_send()
+    sp_qkv.wait_send()
+    for spread in back_q:
+        spread.wait_send()
     ag_one.drain()
     red_mixed.drain()
     red_one.drain()
@@ -1155,20 +1222,25 @@
     steps = 4
     tall, low = rows // steps, shard // steps
 
-    def body(mixed_in, tokens_in, small_in, pin_qkv, own_o, zin_o, pin_f0, pin_f1, mixed, tokens, gains, bias, qkv, o, gate, up, down):
+    heads = q_width // HD
+
+    def body(mixed_in, tokens_in, small_in, pin_q0, pin_q1, own_o, zin_o, *rest):
+        pins, (mixed, tokens, g0, g1, g2, g3, bias, qkv, o, gate, up, down) = rest[: len(parts)], rest[len(parts) :]
         mixed[0] = mixed_in[...]
         tokens[0] = tokens_in[...]
         o[...] = own_o[...].astype(F32) + zin_o[0].astype(F32) + zin_o[1].astype(F32)
-        for k in range(4):
-            gains[0:1, k * shard : (k + 1) * shard] = small_in[k : k + 1, 0:shard]
+        for k, gain in enumerate((g0, g1, g2, g3)):
+            gain[...] = small_in[k : k + 1, 0:shard]
         for k in range(3):
             bias[0:1, k * HD : (k + 1) * HD] = small_in[4 + k : 5 + k, 0:HD]
         for other in range(members):
             for j in range(3):
                 for zh in range(planes):
                     at = j * D + zh * members * HD + other * HD
-                    qkv[:, at : at + HD] = pin_qkv[other, :, j * q_width + zh * HD : j * q_width + (zh + 1) * HD].astype(F32)
-            for pin, width, start in zip((pin_f0, pin_f1), parts, starts):
+                    pin = (pin_q0, pin_q1)[zh // (heads // 2)]
+                    first = qkv_lane(j, zh % (heads // 2), heads)
+                    qkv[:, at : at + HD] = pin[other, :, first : first + HD].astype(F32)
+            for pin, width, start in zip(pins, parts, starts):
                 at = other * f_width + start
                 for k, target in enumerate((gate, up, down)):
                     target[:, at : at + width] = pin[other, :, k * width : (k + 1) * width].astype(F32)
@@ -1178,12 +1250,13 @@
         return pl.BlockSpec(block, lambda i: tuple(i if k == axis else 0 for k in range(len(shape))))
 
     ins = [
-        (got["out_mixed"], 0, tall), (got["out_tokens"], 0, tall), (got["out_small"], None, 0), (got["pin_qkv"], 1, low),
-        (got["own_o"], 0, low), (got["zin_o"], 1, low), (got["pin_f0"], 1, low), (got["pin_f1"], 1, low),
-    ]
+        (got["out_mixed"], 0, tall), (got["out_tokens"], 0, tall), (got["out_small"], None, 0), (got["pin_q0"], 1, low), (got["pin_q1"], 1, low),
+        (got["own_o"], 0, low), (got["zin_o"], 1, low),
+    ] + [(got[f"pin_f{p}"], 1, low) for p in range(len(parts))]
     outs = dict(
         mixed=((1, rows, D), BF, 1, tall), tokens=((1, rows, D), F32, 1, tall),
-        gains=((1, 4 * shard), F32, None, 0), bias=((1, 3 * HD), F32, None, 0),
+        g0=((1, shard), F32, None, 0), g1=((1, shard), F32, None, 0), g2=((1, shard), F32, None, 0), g3=((1, shard), F32, None, 0),
+        bias=((1, 3 * HD), F32, None, 0),
         qkv=((shard, 3 * D), F32, 0, low), o=((shard, D), F32, 0, low),
         gate=((shard, FF), F32, 0, low), up=((shard, FF), F32, 0, low), down=((shard, FF), F32, 0, low),
     )
@@ -1208,16 +1281,13 @@
     q_width = D // members
     f_width = FF // members
     plane_rows = members * shard
-    parts = (384, f_width - 384)
+    parts = (256, 256, f_width - 512)
     dims = (planes, columns, members, rows, shard, q_width, f_width, parts)
-    pieces = jnp.concatenate(
-        [jnp.stack([ln1_gain, ln1_shift, ln2_gain, ln2_shift]), qkv_bias.reshape(3, HD)], axis=0
-    ).astype(F32)
-    small = jnp.pad(pieces, ((0, 1), (0, 128 - HD)))
     inputs = dict(
         in_tokens=(tokens.reshape(rows, D), ANY),
         in_cot=(out_grad.reshape(rows, D), ANY),
-        in_small=(small, VM),
+        in_g0=(ln1_gain.reshape(1, shard), VM), in_g1=(ln1_shift.reshape(1, shard), VM),
+        in_g2=(ln2_gain.reshape(1, shard), VM), in_g3=(ln2_shift.reshape(1, shard), VM), in_bias=(qkv_bias.reshape(1, 3 * HD), VM),
         in_qkv=(qkv_weight, ANY),
         in_o=(out_weight, ANY),
         in_gate=(gate_weight, ANY),
@@ -1230,7 +1300,7 @@
         out_mixed=((rows, D), BF, ANY),
         out_tokens=((rows, D), F32, ANY),
         out_small=((8, 128), F32, ANY),
-        pin_qkv=((members, shard, 3 * q_width), BF, ANY),
+        pin_q0=((members, shard, 3 * q_width // 2), BF, ANY), pin_q1=((members, shard, 3 * q_width // 2), BF, ANY),
         own_o=((shard, D), BF, ANY),
         zin_o=((2, shard, D), BF, ANY),
     )
@@ -1238,12 +1308,13 @@
         outs[f"pin_f{p}"] = ((members, shard, width), BF, ANY)
     final = list(outs)
     spaces = dict(
-        a_one=(total, D),
-        g_qkv=(D, 3 * q_width), g_o=(q_width, D),
-        zin_qkv=(2, plane_rows, 3 * q_width),
-        zx_qkv=(2, plane_rows, 3 * q_width), zx_o=(2, shard, D),
-        zs_qkv=(2, plane_rows, 3 * q_width), zs_o=(2, shard, D),
-    )
+        a_one=(total, D), probs=(total, D),
+        g_o=(q_width, D), zx_o=(2, shard, D), zs_o=(2, shard, D),
+    )
+    for half in range(2):
+        spaces[f"g_q{half}"] = (D, 3 * q_width // 2)
+        for kind in ("zin", "zx", "zs"):
+            spaces[f"{kind}_q{half}"] = (2, plane_rows, 3 * q_width // 2)
     for p, width in enumerate(columns_f):
         spaces[f"w_f{p}"] = spaces[f"g_f{p}"] = (D, width)
         for kind in ("zin", "zx", "zs"):
@@ -1257,6 +1328,7 @@
         w_qkv=VM((D, 3 * q_width), BF), w_o=VM((q_width, D), BF),
         qkv=VM((total, 3 * q_width), BF), att=VM((total, q_width), BF),
         st_qkv=VM((members, shard, 3 * q_width), BF),
+        st_q0=VM((members, shard, 3 * q_width // 2), BF), st_q1=VM((members, shard, 3 * q_width // 2), BF),
         small=VM((planes * members, 8, 128), F32), sg=VM((members, planes, 8, 128), F32),
         sgz=VM((planes - 1, 8, 128), F32), sgs=VM((planes, 8, 128), F32), sgp=VM((members - 1, planes, 8, 128), F32), sgt=VM((8, 128), F32),
         vec=VM((8, D), F32), biases=VM((3 * H, 128), F32), bias=VM((8, 3 * q_width), F32),
@@ -1292,13 +1364,13 @@
     return (
         done["mixed"],
         done["tokens"],
-        done["gains"].reshape(4, shard)[0],
-        done["gains"].reshape(4, shard)[1],
+        done["g0"].reshape(shard),
+        done["g1"].reshape(shard),
         done["qkv"],
         done["bias"].reshape(3 * HD),
         done["o"],
-        done["gains"].reshape(4, shard)[2],
-        done["gains"].reshape(4, shard)[3],
+        done["g2"].reshape(shard),
+        done["g3"].reshape(shard),
         done["gate"],
         done["up"],
         done["down"],

time: 445 us -> 427 us (0.960)
  the two profiles are of different devices: /device:TPU:0 before, /device:TPU:15 now
where the time goes in v1:
time: 427 us; the launch traced here: 418 us
  Pallas kernels  416 us (97%)
    pallas_call x1, Pallas kernels, fast_local(): pl.pallas_call(functools.partial(layer_kernel, dims, list(inputs), list(o...  410 us

profile of v1, /device:TPU:15, one launch (start us, length us, event | category | flops | bytes accessed | tf_op | source)
XLA Modules:
  0.0 418.3 jit_solution(14719367241294703380)
XLA Ops:
  0.6 1.2 reshape.66.refs_6_
  1.9 409.7 %layer.1 = (bf16[128,2048]{1,0:T(8,128)(2,1)}, f32[128,2048]{1,0:T(8,128)}, f32[8,128]{1,0:T(8,128)}, bf16[8,64,384]{2,1,0:T(8,128)(2,1)}, bf16[8,64,384]{2,1,0:...) custom-call(bf16[128,2048]{1,0:T(8,128)(2,1)} %bitcast.11, ...), custom_call_target="tpu_custom_call" | custom-call | flops 41999998976 | bytes 300000000 | tf_op jit(solution)/shard_map/layer/pallas_call | solution.py:1351
  411.6 6.2 %finish.1 = (bf16[1,128,2048]{2,1,0:T(8,128)(2,1)}, f32[1,128,2048]{2,1,0:T(8,128)}, f32[1,64]{1,0:T(1,128)}, f32[1,64]{1,0:T(1,128)}, f32[1,64]{1,0:T(1,128)}, ...) custom-call(bf16[128,2048]{1,0:T(8,128)(2,1)} %get-tuple-element.34., ...), custom_call_target="tpu_custom_call" | custom-call | tf_op jit(solution)/shard_map/finish/pallas_call | solution.py:1263
